TPU v7x, 32 devices: a whole 2x2x4 slice. The times are simulated.
32 devices in a mesh: grp: 2 (over y), freq: 4 (over z), tri: 2 (over x), sta: 2 (over core).
Axes of the slice: x: 2, y: 2, z: 4, core: 2. Of those that a mesh axis runs over, the one named last changes fastest.
Arguments:
- slip: float32 [8, 8192], P(None, ('grp', 'freq', 'tri')), parts along dimension 1, may hold values from 0 to 1
- green: float32 [32, 8, 64, 128], P('freq'), may hold values from -0.09375 to 0.09375
- pattern: int32 [64, 64], P('sta'), may hold values from -1 to 7
- observed: float32 [2, 64, 4096], P(None, ('grp', 'freq'), 'sta'), parts along dimension 1, may hold values from -6 to 6
- adjacency: int32 [3, 2048], P(None, ('freq', 'tri')), may hold values from 0 to 2047, as said below
- smooth_weight: float32 [2], P('grp'), parts along dimension 0, may hold values from 2 to 8
Outputs:
- new_slip: float32 [8, 8192], P(None, ('grp', 'freq', 'tri')), parts along dimension 1
- residual: float32 [2, 64, 4096], P(None, ('grp', 'freq'), 'sta'), parts along dimension 1
There are 2 independent parts, one for each index of `grp`. A program takes and returns all parts, laid end to end along the dimension named above; an argument that names none is the same for every part. Nothing has to cross between parts.
Inputs may be any that keep to these rules, and one draw needn't show every extreme that they name: adjacency[j, t] differs from t by 1 to 256, and adjacency[0, t] differs from t by exactly 256. `pattern`: -1 marks an absent block.
All inputs are finite; a program needn't handle non-finite values.
Results may differ from a plain program's by a relative error of at most 0.000058.
Values sent between devices are 32-bit elements; how exact they have to be, the bound alone decides.
No kernel may reach another device: no remote copies, remote signals or barrier semaphores. Data moves between devices by JAX's collectives and lax.ppermute only.
A program may use at most 64 MiB of HBM per device.

v0:
```python
import math
import jax
import jax.numpy as jnp
from jax import lax
from jax.sharding import PartitionSpec as P

PRECISE = lax.Precision.HIGHEST


def padded_2(shard, sides, width):
    for axis, dim in sides:
        peers, length = (lax.axis_size(axis), shard.shape[dim])
        up = [(i, (i + 1) % peers) for i in range(peers - 1)]
        down = [(j, i) for i, j in up]
        last = lax.slice_in_dim(shard, length - width, length, axis=dim)
        initial = lax.slice_in_dim(shard, 0, width, axis=dim)
        before = lax.ppermute(last, axis, up)
        after = lax.ppermute(initial, axis, down)
        shard = jnp.concatenate([before, shard, after], axis=dim)
    return shard


def phase_tables(first_freq, freq_count, freq_total, windows):
    frequency = jnp.arange(freq_count, dtype=jnp.float32) + first_freq + 1.0
    window = jnp.arange(windows, dtype=jnp.float32) + 0.5
    phases = 4.0 * math.pi / freq_total * frequency[:, None] * window[None, :]
    return (jnp.cos(phases), -jnp.sin(phases))


def apply_green(spectra, green, onehot, block):
    freqs = spectra.shape[1]
    columns = spectra.reshape(2, freqs, -1, block)
    summed = jnp.einsum("skc,rfcx->rfskx", onehot, columns, precision=PRECISE)
    green_real = green[:, :, :, :block]
    green_imag = green[:, :, :, block:]

    def product(left, right):
        return jnp.einsum("fkyx,fskx->fsy", left, right, precision=PRECISE)

    real_part = product(green_real, summed[0]) - product(green_imag, summed[1])
    imag_part = product(green_real, summed[1]) + product(green_imag, summed[0])
    return jnp.stack([real_part, imag_part]).reshape(2, freqs, -1)


def adjoint_green(misfit, green, onehot, block):
    freqs = misfit.shape[1]
    blocks = misfit.reshape(2, freqs, -1, block)
    green_real = green[:, :, :, :block]
    green_imag = green[:, :, :, block:]

    def product(left, right):
        return jnp.einsum("fkyx,fsy->fskx", left, right, precision=PRECISE)

    real_part = product(green_real, blocks[0]) + product(green_imag, blocks[1])
    imag_part = product(green_real, blocks[1]) - product(green_imag, blocks[0])
    result = jnp.einsum(
        "skc,rfskx->rfcx", onehot, jnp.stack([real_part, imag_part]), precision=PRECISE
    )
    return result.reshape(2, freqs, -1)


def local(slip, green, pattern, observed, adjacency, smooth_weight):
    smoothing = smooth_weight[0]
    n_freq = lax.axis_size("freq")
    n_tri = lax.axis_size("tri")
    freq_dev = green.shape[0]
    classes = green.shape[1]
    block = green.shape[2]
    freq_total = freq_dev * n_freq
    windows, columns = slip.shape
    tri_dev = columns // 2
    per_block = columns // block
    station_rows = pattern.shape[0]
    layout = pattern.reshape(station_rows, n_freq, n_tri, per_block)
    layout = lax.dynamic_index_in_dim(layout, lax.axis_index("tri"), 2, keepdims=False)
    layout = layout.reshape(station_rows, n_freq * per_block)
    onehot = (layout[:, None, :] == jnp.arange(classes, dtype=jnp.int32)[None, :, None]).astype(
        jnp.float32
    )
    cos_table, sin_table = phase_tables(0, freq_total, freq_total, windows)

    def to_spectra(field):
        spread = jnp.stack(
            [
                jnp.dot(cos_table, field, precision=PRECISE),
                jnp.dot(sin_table, field, precision=PRECISE),
            ]
        )
        return lax.all_to_all(spread, "freq", split_axis=1, concat_axis=2, tiled=True)

    def predict(field):
        partial_data = apply_green(to_spectra(field), green, onehot, block)
        return lax.psum(partial_data, "tri")

    predicted = predict(slip)
    residual = predicted - observed
    adjoint_part = adjoint_green(residual, green, onehot, block)
    adjoint_part = lax.psum(adjoint_part, "sta")
    by_frequency = lax.all_to_all(adjoint_part, "freq", split_axis=2, concat_axis=1, tiled=True)
    data_grad = jnp.dot(cos_table.T, by_frequency[0], precision=PRECISE) + jnp.dot(
        sin_table.T, by_frequency[1], precision=PRECISE
    )
    padded = padded_2(slip, ((("freq", "tri"), 1),), columns)
    padded_grid = padded.reshape(windows, 3 * tri_dev, 2)
    device_pos = lax.axis_index(("freq", "tri"))
    local_index = adjacency - (device_pos * tri_dev - tri_dev)
    picked = jnp.take(padded_grid, local_index, axis=1)
    neighbour_mean = (picked[:, 0] + picked[:, 1] + picked[:, 2]) / 3.0
    gradient = data_grad + smoothing * (slip - neighbour_mean.reshape(windows, columns))
    numerator = lax.psum(jnp.sum(gradient * gradient), ("freq", "tri"))
    image_data = predict(gradient)
    image_total = lax.psum(jnp.sum(image_data * image_data), ("freq", "sta"))
    denominator = image_total + smoothing * numerator
    step_length = numerator / denominator
    new_slip = jnp.maximum(slip - step_length * gradient, 0.0)
    return (new_slip, residual)


def solution(mesh):
    placed = (
        P(None, ("grp", "freq", "tri")),
        P("freq", None, None, None),
        P("sta", None),
        P(None, ("grp", "freq"), "sta"),
        P(None, ("freq", "tri")),
        P("grp"),
    )
    return jax.shard_map(
        local,
        mesh=mesh,
        in_specs=placed,
        out_specs=(P(None, ("grp", "freq", "tri")), P(None, ("grp", "freq"), "sta")),
        check_vma=False,
    )
```

profile of v0, /device:TPU:0, one launch (start us, length us, event | category | flops | bytes accessed | tf_op | source)
XLA Modules:
  0.0 188.8 jit_solution(9437272294900684459)
XLA Ops:
  7.2 5.0 %collective-permute-start = (f32[8,512]{1,0:T(8,128)}, f32[8,512]{1,0:T(8,128)S(1)}, u32[]{:S(2)}, u32[]{:S(2)}) collective-permute-start(f32[8,512]{1,0:T(8,128)} %param.6), channel_id=1, source_target_pairs={{0,2},{2,4},{4,6},{6,8},{8,10},{10,12},{12,14},{1,3},{3,5},{5,7},{... | collective-permute-start | bytes 49160 | tf_op jit(solution)/shard_map/ppermute | solution.py:17
  16.4 6.9 %all-to-all-start = ((f32[2,32,512]{2,0,1:T(2,128)}), f32[2,32,512]{2,0,1:T(2,128)S(1)}, u32[]{:S(2)}, u32[]{:S(2)}) async-start(f32[2,32,512]{2,0,1:T(2,128)} %copy.59), calls=%async_computation | async-start | bytes 262144 | tf_op jit(solution)/shard_map/all_to_all | solution.py:89
  26.2 3.1 %all-to-all-done = f32[2,32,512]{2,0,1:T(2,128)S(1)} async-done(((f32[2,32,512]{2,0,1:T(2,128)}), f32[2,32,512]{2,0,1:T(2,128)S(1)}, u32[]{:S(2)}, u32[]{:S(2)}) %all-to-all-start) | async-done | bytes 131104 | tf_op jit(solution)/shard_map/all_to_all | solution.py:89
  30.5 1.9 %fusion.43 = f32[8,32,64]{2,1,0:T(8,128)S(1)} fusion(f32[8,8,64,128]{3,2,1,0:T(8,128)S(1)} %copy-done, f32[2,8,32,8,64]{4,2,3,1,0:T(8,128)S(1)} %convolution_bitcast_fusion.1), kind=kOutput, calls=%fused_computation.36 | convolution fusion | flops 100663296 | bytes 3211264 | tf_op jit(solution)/shard_map/fkyx,fskx->fsy/dot_general | solution.py:38
  32.4 1.9 %fusion.46 = f32[8,32,64]{2,1,0:T(8,128)S(1)} fusion(f32[8,8,64,128]{3,2,1,0:T(8,128)S(1)} %copy-done, f32[2,8,32,8,64]{4,2,3,1,0:T(8,128)S(1)} %convolution_bitcast_fusion.1), kind=kOutput, calls=%fused_computation.37 | convolution fusion | flops 100663296 | bytes 3211264 | tf_op jit(solution)/shard_map/fkyx,fskx->fsy/dot_general | solution.py:38
  34.4 2.2 %fusion.76 = f32[8,32,64]{2,1,0:T(8,128)S(1)} fusion(f32[8,32,64]{2,1,0:T(8,128)S(1)} %fusion.43, f32[8,8,64,128]{3,2,1,0:T(8,128)S(1)} %copy-done, f32[2,8,32,8,64]{4,2,3,1,0:T(8,128)S(1)} %convolution_bitcast_fusion.1), kind=kOutput, calls=%fused_computation.47 | convolution fusion | flops 100679680 | bytes 3342336 | tf_op jit(solution)/shard_map/fkyx,fskx->fsy/dot_general | solution.py:38
  36.7 3.4 %fusion.73 = f32[8,32,64]{2,1,0:T(8,128)S(1)} fusion(f32[8,32,64]{2,1,0:T(8,128)S(1)} %fusion.46, f32[8,8,64,128]{3,2,1,0:T(8,128)S(1)} %copy-done, f32[2,8,32,8,64]{4,2,3,1,0:T(8,128)} %copy-done.2), kind=kOutput, calls=%fused_computation.46 | convolution fusion | flops 100679680 | bytes 3276800 | tf_op jit(solution)/shard_map/fkyx,fskx->fsy/dot_general | solution.py:38
  41.4 3.2 %gather_fusion = f32[768,8,2]{1,2,0:T(2,128)} fusion(f32[8,768,2]{0,2,1:T(2,128)S(1)} %bitcast.129, s32[1024]{0:T(1024)S(1)} %pad_clamp_fusion), kind=kCustom, calls=%fused_computation | custom fusion | bytes 101376 | tf_op jit(solution)/shard_map/jit(_take)/gather | solution.py:107
  44.6 1.9 copy.70
  46.5 14.1 %all-reduce.4.cloned.1.call-done = f32[2,8,2048]{2,1,0:T(8,128)} async-done(((f32[2,8,2048]{2,1,0:T(8,128)}), f32[2,8,2048]{2,1,0:T(8,128)}) %all-reduce.4.cloned.1.call-update) | async-done | bytes 131088 | tf_op jit(solution)/shard_map/psum | solution.py:93
  69.7 2.3 %copy.91 = f32[2,8,32,64]{1,0,3,2:T(2,128)} copy(f32[2,8,32,64]{3,2,1,0:T(8,128)S(1)} %fusion.40) | data formatting | bytes 262144 | tf_op jit(solution)/shard_map/reshape | solution.py:59
  72.1 21.3 %all-reduce.6.cloned.1.call-done = f32[2,8,2048]{1,0,2:T(2,128)} async-done(((f32[2,8,2048]{1,0,2:T(2,128)}), f32[2,8,2048]{1,0,2:T(2,128)}) %all-reduce.6.cloned.1.call-update) | async-done | bytes 131088 | tf_op jit(solution)/shard_map/psum | solution.py:98
  93.4 5.6 %reshape.99 = f32[4,1,8192]{2,1,0:T(1,128)} reshape(f32[2048,2,8]{2,1,0:T(2,128)} %bitcast.133) | data formatting | bytes 262144
  99.0 4.9 %all-to-all-start.1 = ((f32[4,1,8192]{2,1,0:T(1,128)}), f32[4,1,8192]{2,1,0:T(1,128)S(1)}, u32[]{:S(2)}, u32[]{:S(2)}) async-start(f32[4,1,8192]{2,1,0:T(1,128)} %reshape.99), calls=%async_computation.1 | async-start | bytes 262144 | tf_op jit(solution)/shard_map/all_to_all | solution.py:99
  104.1 6.1 %all-to-all-done.1 = f32[4,1,8192]{2,1,0:T(1,128)S(1)} async-done(((f32[4,1,8192]{2,1,0:T(1,128)}), f32[4,1,8192]{2,1,0:T(1,128)S(1)}, u32[]{:S(2)}, u32[]{:S(2)}) %all-to-all-start.1) | async-done | bytes 131104 | tf_op jit(solution)/shard_map/all_to_all | solution.py:99
  111.7 4.6 %reshape.100 = f32[2048,2,8]{2,1,0:T(2,128)} reshape(f32[4,8192]{1,0:T(4,128)S(1)} %reduce) | data formatting | bytes 262144
  116.3 2.6 %copy.92 = f32[2,8,4,512]{3,2,1,0:T(4,128)S(1)} copy(f32[2,8,4,512]{1,0,3,2:T(2,128)} %bitcast.132) | data formatting | bytes 262144 | tf_op jit(solution)/shard_map/all_to_all | solution.py:99
  121.0 8.6 %all_to_all.45 = f32[2,32,512]{2,0,1:T(2,128)S(1)} all-to-all(f32[2,32,512]{2,0,1:T(2,128)S(1)} %copy.73), channel_id=1, replica_groups=mesh['grp'=2,'freq'=4,'tri'=2,'sta'=2] {'freq'}, dimensions={1} | all-to-all | bytes 262144 | tf_op jit(solution)/shard_map/all_to_all | solution.py:89
  130.9 1.9 %fusion.49 = f32[8,32,64]{2,1,0:T(8,128)S(1)} fusion(f32[8,8,64,128]{3,2,1,0:T(8,128)S(1)} %copy-done, f32[2,8,32,8,64]{4,2,3,1,0:T(8,128)S(1)} %convolution_bitcast_fusion), kind=kOutput, calls=%fused_computation.38 | convolution fusion | flops 100663296 | bytes 3211264 | tf_op jit(solution)/shard_map/fkyx,fskx->fsy/dot_general | solution.py:38
  132.8 1.9 %fusion.52 = f32[8,32,64]{2,1,0:T(8,128)S(1)} fusion(f32[8,8,64,128]{3,2,1,0:T(8,128)S(1)} %copy-done, f32[2,8,32,8,64]{4,2,3,1,0:T(8,128)S(1)} %convolution_bitcast_fusion), kind=kOutput, calls=%fused_computation.39 | convolution fusion | flops 100663296 | bytes 3211264 | tf_op jit(solution)/shard_map/fkyx,fskx->fsy/dot_general | solution.py:38
  134.8 2.2 %fusion.70 = f32[8,32,64]{2,1,0:T(8,128)S(1)} fusion(f32[8,32,64]{2,1,0:T(8,128)S(1)} %fusion.49, f32[8,8,64,128]{3,2,1,0:T(8,128)S(1)} %copy-done, f32[2,8,32,8,64]{4,2,3,1,0:T(8,128)S(1)} %convolution_bitcast_fusion), kind=kOutput, calls=%fused_computation.45 | convolution fusion | flops 100679680 | bytes 3342336 | tf_op jit(solution)/shard_map/fkyx,fskx->fsy/dot_general | solution.py:38
  137.0 3.4 %fusion.67 = f32[8,32,64]{2,1,0:T(8,128)S(1)} fusion(f32[8,32,64]{2,1,0:T(8,128)S(1)} %fusion.52, f32[8,8,64,128]{3,2,1,0:T(8,128)S(1)} %copy-done, f32[2,8,32,8,64]{4,2,3,1,0:T(8,128)} %copy-done.1), kind=kOutput, calls=%fused_computation.44 | convolution fusion | flops 100679680 | bytes 3276800 | tf_op jit(solution)/shard_map/fkyx,fskx->fsy/dot_general | solution.py:38
  141.2 20.3 %psum.37 = f32[]{:T(128)} all-reduce(f32[]{:T(128)} %get-tuple-element.8), channel_id=1, replica_groups=mesh['grp'=2,'freq'=4,'tri'=2,'sta'=2] {'freq','tri'}, use_global_device_ids=true, to_apply=%region_3.4 | all-reduce | flops 1 | bytes 8 | tf_op jit(solution)/shard_map/psum | solution.py:110
  164.1 16.4 %psum.39 = f32[]{:T(128)} all-reduce(f32[]{:T(128)} %multiply_reduce_fusion), channel_id=1, replica_groups=mesh['grp'=2,'freq'=4,'tri'=2,'sta'=2] {'freq','sta'}, use_global_device_ids=true, to_apply=%region_6.7 | all-reduce | flops 1 | bytes 8 | tf_op jit(solution)/shard_map/psum | solution.py:112
  (88 shorter events, 26.5 us)
Async XLA Ops:
  7.2 23.3 %copy-start = (f32[8,8,64,128]{3,2,1,0:T(8,128)S(1)}, f32[8,8,64,128]{3,2,1,0:T(8,128)}, u32[]{:S(2)}) copy-start(f32[8,8,64,128]{3,2,1,0:T(8,128)} %param.7) | copy-start | bytes 6291460
  7.2 33.9 %collective-permute-start = (f32[8,512]{1,0:T(8,128)}, f32[8,512]{1,0:T(8,128)S(1)}, u32[]{:S(2)}, u32[]{:S(2)}) collective-permute-start(f32[8,512]{1,0:T(8,128)} %param.6), channel_id=1, source_target_pairs={{0,2},{2,4},{4,6},{6,8},{8,10},{10,12},{12,14},{1,3},{3,5},{5,7},{... | collective-permute-start | bytes 49160 | tf_op jit(solution)/shard_map/ppermute | solution.py:17
  12.2 28.9 %collective-permute-start.1 = (f32[8,512]{1,0:T(8,128)}, f32[8,512]{1,0:T(8,128)S(1)}, u32[]{:S(2)}, u32[]{:S(2)}) collective-permute-start(f32[8,512]{1,0:T(8,128)} %param.6), channel_id=1, source_target_pairs={{2,0},{4,2},{6,4},{8,6},{10,8},{12,10},{14,12},{3,1},{5,3},{7,5},{... | collective-permute-start | bytes 49160 | tf_op jit(solution)/shard_map/ppermute | solution.py:18
  13.5 1.1 copy-start.9
  13.5 1.1 copy-start.11
  16.4 12.8 %all-to-all-start = ((f32[2,32,512]{2,0,1:T(2,128)}), f32[2,32,512]{2,0,1:T(2,128)S(1)}, u32[]{:S(2)}, u32[]{:S(2)}) async-start(f32[2,32,512]{2,0,1:T(2,128)} %copy.59), calls=%async_computation | async-start | bytes 262144 | tf_op jit(solution)/shard_map/all_to_all | solution.py:89
  23.3 37.2 %all-reduce.4.cloned.1.call-start = ((), (), s32[]{:S(2)}) async-start(), calls=%async_computation.3 | async-start | bytes 262144 | tf_op jit(solution)/shard_map/psum | solution.py:93
  25.5 6.9 %copy-start.5 = (s32[32,32]{1,0:T(8,128)}, s32[32,32]{1,0:T(8,128)S(1)}, u32[]{:S(2)}) copy-start(s32[32,32]{1,0:T(8,128)S(1)} %copy.62) | copy-start | bytes 12292
  30.5 3.9 %copy-start.2 = (f32[2,8,32,8,64]{4,2,3,1,0:T(8,128)}, f32[2,8,32,8,64]{4,2,3,1,0:T(8,128)S(1)}, u32[]{:S(2)}) copy-start(f32[2,8,32,8,64]{4,2,3,1,0:T(8,128)S(1)} %convolution_bitcast_fusion.1) | copy-start | bytes 3145732
  36.6 4.5 %copy-start.4 = (f32[8,512]{1,0:T(8,128)S(1)}, f32[8,512]{1,0:T(8,128)}, u32[]{:S(2)}) copy-start(f32[8,512]{1,0:T(8,128)} %param.6) | copy-start | bytes 49156
  40.8 52.6 %all-reduce.6.cloned.1.call-start = ((), (), s32[]{:S(2)}) async-start(), calls=%async_computation.4 | async-start | bytes 4194304 | tf_op jit(solution)/shard_map/psum | solution.py:98
  41.4 19.2 %copy-start.8 = (f32[2,8,2048]{2,1,0:T(8,128)S(1)}, f32[2,8,2048]{2,1,0:T(8,128)}, u32[]{:S(2)}) copy-start(f32[2,8,2048]{2,1,0:T(8,128)} %param.9) | copy-start | bytes 393220
  61.5 4.8 %copy-start.3 = (f32[2,8,2048]{2,1,0:T(8,128)}, f32[2,8,2048]{2,1,0:T(8,128)S(1)}, u32[]{:S(2)}) copy-start(f32[2,8,2048]{2,1,0:T(8,128)S(1)} %sub.28) | copy-start | bytes 393220
  67.5 1.2 copy-start.6
  69.7 2.3 %copy-start.7 = (f32[3,256,8,2]{1,2,3,0:T(8,128)S(1)}, f32[3,256,8,2]{1,2,3,0:T(8,128)}, u32[]{:S(2)}) copy-start(f32[3,256,8,2]{1,2,3,0:T(8,128)} %copy.70) | copy-start | bytes 147460
  69.7 2.3 %copy-start.13 = (pred[3,256]{1,0:T(4,128)(4,1)S(1)}, pred[3,256]{1,0:T(4,128)(4,1)}, u32[]{:S(2)}) copy-start(pred[3,256]{1,0:T(4,128)(4,1)} %get-tuple-element.2) | copy-start | bytes 2308
  99.0 11.2 %all-to-all-start.1 = ((f32[4,1,8192]{2,1,0:T(1,128)}), f32[4,1,8192]{2,1,0:T(1,128)S(1)}, u32[]{:S(2)}, u32[]{:S(2)}) async-start(f32[4,1,8192]{2,1,0:T(1,128)} %reshape.99), calls=%async_computation.1 | async-start | bytes 262144 | tf_op jit(solution)/shard_map/all_to_all | solution.py:99
  103.8 58.1 %all-reduce.8.cloned.1.call-start = ((), (), s32[]{:S(2)}) async-start(), calls=%async_computation.5 | async-start | bytes 262144 | tf_op jit(solution)/shard_map/psum | solution.py:93
  111.7 7.3 %copy-start.10 = (f32[32]{0:T(128)S(1)}, f32[32]{0:T(128)}, u32[]{:S(2)}) copy-start(f32[32]{0:T(128)} %copy-done.9) | copy-start | bytes 388
  111.7 7.3 %copy-start.12 = (f32[8]{0:T(128)S(1)}, f32[8]{0:T(128)}, u32[]{:S(2)}) copy-start(f32[8]{0:T(128)} %copy-done.11) | copy-start | bytes 100
  130.9 3.9 %copy-start.1 = (f32[2,8,32,8,64]{4,2,3,1,0:T(8,128)}, f32[2,8,32,8,64]{4,2,3,1,0:T(8,128)S(1)}, u32[]{:S(2)}) copy-start(f32[2,8,32,8,64]{4,2,3,1,0:T(8,128)S(1)} %convolution_bitcast_fusion) | copy-start | bytes 3145732
Sparse Core Ops, SparseCore 0:
  40.9 19.5 all-reduce.3
  72.1 21.2 all-reduce.5
  141.3 20.5 all-reduce.7
where the time goes:
time: 190 us; the launch traced here: 189 us
  blocking collectives  45.3 us (24%)
  waiting for transfers between devices  45.1 us (24%)
  matrix products  31.2 us (16%)
  local copies, waits for them, and re-layouts  25.5 us (13%)
  starting transfers between devices  18.3 us (10%)
  between operations  16.7 us (9%)
  other arithmetic  6.71 us (4%)
    psum x1, waiting for transfers between devices, local(): adjoint_part = lax.psum(adjoint_part, 'sta')  21.3 us
    psum x1, blocking collectives, local(): numerator = lax.psum(jnp.sum(gradient * gradient), ('freq', 'tri'))  20.3 us
    dot_general x8, matrix products, product(): return jnp.einsum('fkyx,fskx->fsy', left, right, precision=PRECISE)  18.8 us
    psum x1, blocking collectives, local(): image_total = lax.psum(jnp.sum(image_data * image_data), ('freq', 'sta'))  16.4 us
    psum x2, waiting for transfers between devices, predict(): return lax.psum(partial_data, 'tri')  14.5 us
    unnamed x31, local copies, waits for them, and re-layouts  11 us
    all_to_all x1, blocking collectives, to_spectra(): lax.all_to_all(spread, 'freq', split_axis=1, concat_axis=2, tiled=True)  8.61 us
    all_to_all x1, starting transfers between devices, to_spectra(): lax.all_to_all(spread, 'freq', split_axis=1, concat_axis=2, tiled=True)  6.93 us
  transfers between devices with their start and end apart: 7, of which 5 were waited for; matrix products, arithmetic and copies ran while one was open for 12% of the time, Pallas kernels for 0%

commit v1 on v0

--- a/solution.py
+++ b/solution.py
@@ -95,7 +95,8 @@
     predicted = predict(slip)
     residual = predicted - observed
     adjoint_part = adjoint_green(residual, green, onehot, block)
-    adjoint_part = lax.psum(adjoint_part, "sta")
+    shards = lax.all_gather(adjoint_part, "sta", axis=0, tiled=False)
+    adjoint_part = shards.sum(axis=0)
     by_frequency = lax.all_to_all(adjoint_part, "freq", split_axis=2, concat_axis=1, tiled=True)
     data_grad = jnp.dot(cos_table.T, by_frequency[0], precision=PRECISE) + jnp.dot(
         sin_table.T, by_frequency[1], precision=PRECISE

time: 190 us -> 173 us (0.911)
  waiting for transfers between devices: 45.1 us -> 28.1 us
    psum x1 -> x0, waiting for transfers between devices: 21.3 us -> none  [local(): adjoint_part = lax.psum(adjoint_part, 'sta')]
    psum x2, waiting for transfers between devices: 14.5 us -> 22.1 us  [predict(): return lax.psum(partial_data, 'tri')]
    all_to_all x1, waiting for transfers between devices: 3.07 us -> 0.01 us  [to_spectra(): lax.all_to_all(spread, 'freq', split_axis=1, concat_axis=2, tiled=True)]
    reshape x1 -> x0, local copies, waits for them, and re-layouts: 2.29 us -> none  [adjoint_green(): return result.reshape(2, freqs, -1)]
    reduce_sum x0 -> x1, local copies, waits for them, and re-layouts: none -> 2.25 us  [local(): adjoint_part = shards.sum(axis=0)]
    all_gather x0 -> x1, blocking collectives: none -> 1.99 us  [local(): shards = lax.all_gather(adjoint_part, 'sta', axis=0, tiled=False)]
    gather x2, local copies, waits for them, and re-layouts: 5.11 us -> 3.15 us  [local(): picked = jnp.take(padded_grid, local_index, axis=1)]
    unnamed x31 -> x25, local copies, waits for them, and re-layouts: 11 us -> 11 us
  transfers between devices with their start and end apart: 7 -> 6, of which waited for: 5 -> 3; matrix products, arithmetic and copies ran while one was open for 12% -> 6% of each run, Pallas kernels for 0% -> 0%
where the time goes in v1:
time: 173 us; the launch traced here: 172 us
  blocking collectives  46.2 us (27%)
  matrix products  31.5 us (18%)
  waiting for transfers between devices  28.1 us (16%)
  local copies, waits for them, and re-layouts  23.7 us (14%)
  starting transfers between devices  17.7 us (10%)
  between operations  17.1 us (10%)
  other arithmetic  7.51 us (4%)
    psum x2, waiting for transfers between devices, predict(): return lax.psum(partial_data, 'tri')  22.1 us
    psum x1, blocking collectives, local(): numerator = lax.psum(jnp.sum(gradient * gradient), ('freq', 'tri'))  19.2 us
    dot_general x8, matrix products, product(): return jnp.einsum('fkyx,fskx->fsy', left, right, precision=PRECISE)  18.9 us
    psum x1, blocking collectives, local(): image_total = lax.psum(jnp.sum(image_data * image_data), ('freq', 'sta'))  16.4 us
    unnamed x25, local copies, waits for them, and re-layouts  11 us
    all_to_all x1, blocking collectives, to_spectra(): lax.all_to_all(spread, 'freq', split_axis=1, concat_axis=2, tiled=True)  8.6 us
    all_to_all x1, starting transfers between devices, to_spectra(): lax.all_to_all(spread, 'freq', split_axis=1, concat_axis=2, tiled=True)  6.93 us
    all_to_all x1, waiting for transfers between devices, local(): lax.all_to_all(adjoint_part, 'freq', split_axis=2, concat_axis=1, tiled=T...  5.95 us
  transfers between devices with their start and end apart: 6, of which 3 were waited for; matrix products, arithmetic and copies ran while one was open for 6% of the time, Pallas kernels for 0%

profile of v1, /device:TPU:0, one launch (start us, length us, event | category | flops | bytes accessed | tf_op | source)
XLA Modules:
  0.0 171.8 jit_solution(1240194296911120453)
XLA Ops:
  7.2 4.8 %collective-permute-start = (f32[8,512]{1,0:T(8,128)}, f32[8,512]{1,0:T(8,128)S(1)}, u32[]{:S(2)}, u32[]{:S(2)}) collective-permute-start(f32[8,512]{1,0:T(8,128)} %param.6), channel_id=1, source_target_pairs={{0,2},{2,4},{4,6},{6,8},{8,10},{10,12},{12,14},{1,3},{3,5},{5,7},{... | collective-permute-start | bytes 49160 | tf_op jit(solution)/shard_map/ppermute | solution.py:17
  16.2 6.9 %all-to-all-start = ((f32[2,32,512]{2,0,1:T(2,128)}), f32[2,32,512]{2,0,1:T(2,128)S(1)}, u32[]{:S(2)}, u32[]{:S(2)}) async-start(f32[2,32,512]{2,0,1:T(2,128)} %copy.71), calls=%async_computation | async-start | bytes 262144 | tf_op jit(solution)/shard_map/all_to_all | solution.py:89
  26.4 2.8 %gather_fusion = f32[768,8,2]{1,2,0:T(2,128)S(1)} fusion(f32[8,768,2]{0,2,1:T(2,128)S(1)} %bitcast.130, s32[1024]{0:T(1024)S(1)} %pad_clamp_fusion), kind=kCustom, calls=%fused_computation | custom fusion | bytes 101376 | tf_op jit(solution)/shard_map/jit(_take)/gather | solution.py:108
  30.9 1.9 %fusion.43 = f32[8,32,64]{2,1,0:T(8,128)S(1)} fusion(f32[8,8,64,128]{3,2,1,0:T(8,128)S(1)} %copy-done, f32[2,8,32,8,64]{4,2,3,1,0:T(8,128)S(1)} %convolution_bitcast_fusion.1), kind=kOutput, calls=%fused_computation.36 | convolution fusion | flops 100663296 | bytes 3211264 | tf_op jit(solution)/shard_map/fkyx,fskx->fsy/dot_general | solution.py:38
  32.8 1.9 %fusion.46 = f32[8,32,64]{2,1,0:T(8,128)S(1)} fusion(f32[8,8,64,128]{3,2,1,0:T(8,128)S(1)} %copy-done, f32[2,8,32,8,64]{4,2,3,1,0:T(8,128)S(1)} %convolution_bitcast_fusion.1), kind=kOutput, calls=%fused_computation.37 | convolution fusion | flops 100663296 | bytes 3211264 | tf_op jit(solution)/shard_map/fkyx,fskx->fsy/dot_general | solution.py:38
  34.8 2.2 %fusion.76 = f32[8,32,64]{2,1,0:T(8,128)S(1)} fusion(f32[8,32,64]{2,1,0:T(8,128)S(1)} %fusion.43, f32[8,8,64,128]{3,2,1,0:T(8,128)S(1)} %copy-done, f32[2,8,32,8,64]{4,2,3,1,0:T(8,128)S(1)} %convolution_bitcast_fusion.1), kind=kOutput, calls=%fused_computation.47 | convolution fusion | flops 100679680 | bytes 3342336 | tf_op jit(solution)/shard_map/fkyx,fskx->fsy/dot_general | solution.py:38
  37.1 3.4 %fusion.73 = f32[8,32,64]{2,1,0:T(8,128)S(1)} fusion(f32[8,32,64]{2,1,0:T(8,128)S(1)} %fusion.46, f32[8,8,64,128]{3,2,1,0:T(8,128)S(1)} %copy-done, f32[2,8,32,8,64]{4,2,3,1,0:T(8,128)} %copy-done.2), kind=kOutput, calls=%fused_computation.46 | convolution fusion | flops 100679680 | bytes 3276800 | tf_op jit(solution)/shard_map/fkyx,fskx->fsy/dot_general | solution.py:38
  41.9 21.5 %all-reduce.3.cloned.1.call-done = f32[2,8,2048]{2,1,0:T(8,128)} async-done(((f32[2,8,2048]{2,1,0:T(8,128)}), f32[2,8,2048]{2,1,0:T(8,128)}) %all-reduce.3.cloned.1.call-update) | async-done | bytes 131088 | tf_op jit(solution)/shard_map/psum | solution.py:93
  67.6 1.6 fusion.8
  72.8 2.0 %all_gather.3 = f32[2,2,8,2048]{3,2,1,0:T(8,128)S(1)} all-gather(f32[1,2,8,2048]{3,2,1,0:T(8,128)S(1)} %all_gather_reshape.3), channel_id=1, replica_groups=mesh['grp'=2,'freq'=4,'tri'=2,'sta'=2] {'sta'}, dimensions={0}, use_global_device_ids=true | all-gather | bytes 393216 | tf_op jit(solution)/shard_map/all_gather | solution.py:98
  74.8 2.2 %copy.76 = f32[2,8,2048]{1,0,2:T(2,128)} copy(f32[2,8,2048]{2,1,0:T(8,128)S(1)} %reduce_sum.27) | data formatting | bytes 262144 | tf_op jit(solution)/shard_map/reduce_sum | solution.py:99
  77.1 5.6 %reshape.95 = f32[4,1,8192]{2,1,0:T(1,128)} reshape(f32[2048,2,8]{2,1,0:T(2,128)} %bitcast.132) | data formatting | bytes 262144
  82.6 4.6 %all-to-all-start.1 = ((f32[4,1,8192]{2,1,0:T(1,128)}), f32[4,1,8192]{2,1,0:T(1,128)S(1)}, u32[]{:S(2)}, u32[]{:S(2)}) async-start(f32[4,1,8192]{2,1,0:T(1,128)} %reshape.95), calls=%async_computation.1 | async-start | bytes 262144 | tf_op jit(solution)/shard_map/all_to_all | solution.py:100
  87.5 5.9 %all-to-all-done.1 = f32[4,1,8192]{2,1,0:T(1,128)S(1)} async-done(((f32[4,1,8192]{2,1,0:T(1,128)}), f32[4,1,8192]{2,1,0:T(1,128)S(1)}, u32[]{:S(2)}, u32[]{:S(2)}) %all-to-all-start.1) | async-done | bytes 131104 | tf_op jit(solution)/shard_map/all_to_all | solution.py:100
  95.0 4.5 %reshape.96 = f32[2048,2,8]{2,1,0:T(2,128)} reshape(f32[4,8192]{1,0:T(4,128)S(1)} %reduce) | data formatting | bytes 262144
  99.5 2.6 %copy.103 = f32[2,8,4,512]{3,2,1,0:T(4,128)S(1)} copy(f32[2,8,4,512]{1,0,3,2:T(2,128)} %bitcast.133) | data formatting | bytes 262144 | tf_op jit(solution)/shard_map/all_to_all | solution.py:100
  104.4 8.6 %all_to_all.45 = f32[2,32,512]{2,0,1:T(2,128)S(1)} all-to-all(f32[2,32,512]{2,0,1:T(2,128)S(1)} %copy.85), channel_id=1, replica_groups=mesh['grp'=2,'freq'=4,'tri'=2,'sta'=2] {'freq'}, dimensions={1} | all-to-all | bytes 262144 | tf_op jit(solution)/shard_map/all_to_all | solution.py:89
  114.2 1.9 %fusion.49 = f32[8,32,64]{2,1,0:T(8,128)S(1)} fusion(f32[8,8,64,128]{3,2,1,0:T(8,128)S(1)} %copy-done, f32[2,8,32,8,64]{4,2,3,1,0:T(8,128)S(1)} %convolution_bitcast_fusion), kind=kOutput, calls=%fused_computation.38 | convolution fusion | flops 100663296 | bytes 3211264 | tf_op jit(solution)/shard_map/fkyx,fskx->fsy/dot_general | solution.py:38
  116.1 1.9 %fusion.52 = f32[8,32,64]{2,1,0:T(8,128)S(1)} fusion(f32[8,8,64,128]{3,2,1,0:T(8,128)S(1)} %copy-done, f32[2,8,32,8,64]{4,2,3,1,0:T(8,128)S(1)} %convolution_bitcast_fusion), kind=kOutput, calls=%fused_computation.39 | convolution fusion | flops 100663296 | bytes 3211264 | tf_op jit(solution)/shard_map/fkyx,fskx->fsy/dot_general | solution.py:38
  118.1 2.2 %fusion.70 = f32[8,32,64]{2,1,0:T(8,128)S(1)} fusion(f32[8,32,64]{2,1,0:T(8,128)S(1)} %fusion.49, f32[8,8,64,128]{3,2,1,0:T(8,128)S(1)} %copy-done, f32[2,8,32,8,64]{4,2,3,1,0:T(8,128)S(1)} %convolution_bitcast_fusion), kind=kOutput, calls=%fused_computation.45 | convolution fusion | flops 100679680 | bytes 3342336 | tf_op jit(solution)/shard_map/fkyx,fskx->fsy/dot_general | solution.py:38
  120.4 3.4 %fusion.67 = f32[8,32,64]{2,1,0:T(8,128)S(1)} fusion(f32[8,32,64]{2,1,0:T(8,128)S(1)} %fusion.52, f32[8,8,64,128]{3,2,1,0:T(8,128)S(1)} %copy-done, f32[2,8,32,8,64]{4,2,3,1,0:T(8,128)} %copy-done.1), kind=kOutput, calls=%fused_computation.44 | convolution fusion | flops 100679680 | bytes 3276800 | tf_op jit(solution)/shard_map/fkyx,fskx->fsy/dot_general | solution.py:38
  124.5 19.2 %psum.29 = f32[]{:T(128)} all-reduce(f32[]{:T(128)} %get-tuple-element.8), channel_id=1, replica_groups=mesh['grp'=2,'freq'=4,'tri'=2,'sta'=2] {'freq','tri'}, use_global_device_ids=true, to_apply=%region_3.4 | all-reduce | flops 1 | bytes 8 | tf_op jit(solution)/shard_map/psum | solution.py:111
  144.3 1.6 multiply_reduce_fusion
  146.6 16.4 %psum.31 = f32[]{:T(128)} all-reduce(f32[]{:T(128)} %multiply_reduce_fusion), channel_id=1, replica_groups=mesh['grp'=2,'freq'=4,'tri'=2,'sta'=2] {'freq','sta'}, use_global_device_ids=true, to_apply=%region_6.7 | all-reduce | flops 1 | bytes 8 | tf_op jit(solution)/shard_map/psum | solution.py:113
  (82 shorter events, 24.7 us)
Async XLA Ops:
  7.2 18.3 %collective-permute-start = (f32[8,512]{1,0:T(8,128)}, f32[8,512]{1,0:T(8,128)S(1)}, u32[]{:S(2)}, u32[]{:S(2)}) collective-permute-start(f32[8,512]{1,0:T(8,128)} %param.6), channel_id=1, source_target_pairs={{0,2},{2,4},{4,6},{6,8},{8,10},{10,12},{12,14},{1,3},{3,5},{5,7},{... | collective-permute-start | bytes 49160 | tf_op jit(solution)/shard_map/ppermute | solution.py:17
  12.0 13.4 %collective-permute-start.1 = (f32[8,512]{1,0:T(8,128)}, f32[8,512]{1,0:T(8,128)S(1)}, u32[]{:S(2)}, u32[]{:S(2)}) collective-permute-start(f32[8,512]{1,0:T(8,128)} %param.6), channel_id=1, source_target_pairs={{2,0},{4,2},{6,4},{8,6},{10,8},{12,10},{14,12},{3,1},{5,3},{7,5},{... | collective-permute-start | bytes 49160 | tf_op jit(solution)/shard_map/ppermute | solution.py:18
  13.3 1.1 copy-start.7
  13.4 1.1 copy-start.9
  16.2 13.4 %all-to-all-start = ((f32[2,32,512]{2,0,1:T(2,128)}), f32[2,32,512]{2,0,1:T(2,128)S(1)}, u32[]{:S(2)}, u32[]{:S(2)}) async-start(f32[2,32,512]{2,0,1:T(2,128)} %copy.71), calls=%async_computation | async-start | bytes 262144 | tf_op jit(solution)/shard_map/all_to_all | solution.py:89
  23.2 40.2 %all-reduce.3.cloned.1.call-start = ((), (), s32[]{:S(2)}) async-start(), calls=%async_computation.3 | async-start | bytes 262144 | tf_op jit(solution)/shard_map/psum | solution.py:93
  29.3 1.6 copy-start
  30.9 3.9 %copy-start.2 = (f32[2,8,32,8,64]{4,2,3,1,0:T(8,128)}, f32[2,8,32,8,64]{4,2,3,1,0:T(8,128)S(1)}, u32[]{:S(2)}) copy-start(f32[2,8,32,8,64]{4,2,3,1,0:T(8,128)S(1)} %convolution_bitcast_fusion.1) | copy-start | bytes 3145732
  37.1 26.4 %copy-start.6 = (f32[2,8,2048]{2,1,0:T(8,128)S(1)}, f32[2,8,2048]{2,1,0:T(8,128)}, u32[]{:S(2)}) copy-start(f32[2,8,2048]{2,1,0:T(8,128)} %param.9) | copy-start | bytes 393220
  64.3 4.8 %copy-start.3 = (f32[2,8,2048]{2,1,0:T(8,128)}, f32[2,8,2048]{2,1,0:T(8,128)S(1)}, u32[]{:S(2)}) copy-start(f32[2,8,2048]{2,1,0:T(8,128)S(1)} %sub.28) | copy-start | bytes 393220
  74.8 12.4 %copy-start.5 = (f32[8,3,256,2]{2,0,3,1:T(8,128)S(1)}, f32[8,3,256,2]{2,0,3,1:T(8,128)}, u32[]{:S(2)}) copy-start(f32[8,3,256,2]{2,0,3,1:T(8,128)} %select_bitcast_fusion) | copy-start | bytes 147460
  82.6 10.8 %all-to-all-start.1 = ((f32[4,1,8192]{2,1,0:T(1,128)}), f32[4,1,8192]{2,1,0:T(1,128)S(1)}, u32[]{:S(2)}, u32[]{:S(2)}) async-start(f32[4,1,8192]{2,1,0:T(1,128)} %reshape.95), calls=%async_computation.1 | async-start | bytes 262144 | tf_op jit(solution)/shard_map/all_to_all | solution.py:100
  87.2 57.0 %all-reduce.5.cloned.1.call-start = ((), (), s32[]{:S(2)}) async-start(), calls=%async_computation.4 | async-start | bytes 262144 | tf_op jit(solution)/shard_map/psum | solution.py:93
  94.9 7.3 %copy-start.8 = (f32[32]{0:T(128)S(1)}, f32[32]{0:T(128)}, u32[]{:S(2)}) copy-start(f32[32]{0:T(128)} %copy-done.7) | copy-start | bytes 388
  95.0 7.3 %copy-start.10 = (f32[8]{0:T(128)S(1)}, f32[8]{0:T(128)}, u32[]{:S(2)}) copy-start(f32[8]{0:T(128)} %copy-done.9) | copy-start | bytes 100
  95.0 7.6 %copy-start.4 = (f32[8,512]{1,0:T(8,128)S(1)}, f32[8,512]{1,0:T(8,128)}, u32[]{:S(2)}) copy-start(f32[8,512]{1,0:T(8,128)} %param.6) | copy-start | bytes 49156
  114.2 3.9 %copy-start.1 = (f32[2,8,32,8,64]{4,2,3,1,0:T(8,128)}, f32[2,8,32,8,64]{4,2,3,1,0:T(8,128)S(1)}, u32[]{:S(2)}) copy-start(f32[2,8,32,8,64]{4,2,3,1,0:T(8,128)S(1)} %convolution_bitcast_fusion) | copy-start | bytes 3145732
Sparse Core Ops, SparseCore 0:
  41.4 21.9 all-reduce.2
  124.6 19.6 all-reduce.4
